TPU v7x, 512 devices: a whole 4x4x16 slice. The times are simulated.
512 devices in a mesh: sec: 128 (over y, z, core), tile: 4 (over x).
Axes of the slice: x: 4, y: 4, z: 16, core: 2. Of those that a mesh axis runs over, the one named last changes fastest.
Arguments:
- node_flow: float32 [128, 2, 256, 512], P('sec', None, 'tile'), may hold values from -6 to 6
- classes: int32 [128, 256, 512], P('sec', 'tile'), may hold values from 0 to 7
- table: float32 [8], replicated, may hold values from 0.3 to 2.5
- z_couple: float32 [128], replicated, may hold values from 22 to 30
- match_dest: int32 [131072, 1], P(('sec', 'tile')), may hold values from 0 to 127; in each aligned block of 256 rows (0 to 255, 256 to 511, ...) at most 4 rows name the same one
- match_slot: int32 [131072], P(('sec', 'tile')), may hold values from 0 to 255
- match_vectors: float32 [131072, 256], P(('sec', 'tile')), may hold values from -6 to 6
Outputs:
- aligned: float32 [128, 2, 256, 512], P('sec', None, 'tile')
Inputs may be any that keep to these rules, and one draw needn't show every extreme that they name: `match_dest`: among the 256 rows of one device no value occurs more than 4 times; one value occurs exactly 4 times.
All inputs are finite; a program needn't handle non-finite values.
Results may differ from a plain program's by a relative error of at most 0.00026.
Values sent between devices are 32-bit elements; how exact they have to be, the bound alone decides.
A program may use at most 192 MiB of HBM per device.

v0:
```python
import jax
import jax.numpy as jnp
from jax import lax
from jax.sharding import PartitionSpec as P

ROUNDS = 2
ISTEPS = 2


relax_rate = 0.05


def with_halo(value, sides, width):
    for axis, dim in sides:
        size, length = (lax.axis_size(axis), value.shape[dim])
        up = [(i, (i + 1) % size) for i in range(size - 1)]
        down = [(j, i) for i, j in up]
        last = lax.slice_in_dim(value, length - width, length, axis=dim)
        leading = lax.slice_in_dim(value, 0, width, axis=dim)
        before = lax.ppermute(last, axis, up)
        after = lax.ppermute(leading, axis, down)
        value = jnp.concatenate([before, value, after], axis=dim)
    return value


def stiffness_map(classes, table):
    result = jnp.zeros(classes.shape, table.dtype)
    for level in range(table.shape[0]):
        result = result + jnp.where(classes == level, table[level], jnp.zeros((), table.dtype))
    return result


def band_coefs(z_couple):
    before = jnp.concatenate([jnp.zeros((1,), z_couple.dtype), z_couple[:-1]])
    lower = -before
    diagonal = 1.0 + z_couple + before
    upper = jnp.concatenate([-z_couple[:-1], jnp.zeros((1,), z_couple.dtype)])
    return (lower, diagonal, upper)


def plane_step(field, stiffness, pulled, counts):
    padded = with_halo(field, (("tile", 2),), 1)
    padded = jnp.pad(padded, ((0, 0), (0, 0), (0, 0), (1, 1)))
    laplace = (
        padded[:, :, 2:, 1:-1]
        + padded[:, :, :-2, 1:-1]
        + padded[:, :, 1:-1, 2:]
        + padded[:, :, 1:-1, :-2]
        - 4.0 * field
    )
    return field + relax_rate * (stiffness[:, None] * laplace + (pulled - counts[:, None] * field))


def local(node_flow, classes, table, z_couple, match_dest, match_slot, match_vectors):
    sec_dev, comps, rows_dev, width = node_flow.shape
    n_sec = lax.axis_size("sec")
    tile_len = match_vectors.shape[1] // comps
    per_row = width // tile_len
    slots_dev = sec_dev * rows_dev * per_row
    matches_dev = match_vectors.shape[0]
    capacity = 2 * (matches_dev // n_sec)
    highest = lax.Precision.HIGHEST
    targets = match_dest[:, 0]
    target_hot = (targets[:, None] == jnp.arange(n_sec, dtype=jnp.int32)[None, :]).astype(jnp.int32)
    earlier_hits = jnp.cumsum(target_hot, axis=0) - target_hot
    slot_order = jnp.sum(earlier_hits * target_hot, axis=1)
    position = targets * capacity + slot_order
    place_hot = (
        jnp.arange(n_sec * capacity, dtype=jnp.int32)[:, None] == position[None, :]
    ).astype(jnp.float32)
    send_rows = jnp.dot(place_hot, match_vectors, precision=highest).reshape(
        n_sec, capacity, comps * tile_len
    )
    send_slots = jnp.dot(
        place_hot, (match_slot + 1).astype(jnp.float32), precision=highest
    ).reshape(n_sec, capacity)
    got_rows, got_slots = (
        lax.all_to_all(send_rows, "sec", split_axis=0, concat_axis=0, tiled=True),
        lax.all_to_all(send_slots, "sec", split_axis=0, concat_axis=0, tiled=True),
    )
    slot_ids = got_slots.reshape(-1).astype(jnp.int32) - 1
    slot_hot = (jnp.arange(slots_dev, dtype=jnp.int32)[:, None] == slot_ids[None, :]).astype(
        jnp.float32
    )
    pulled = jnp.dot(
        slot_hot, got_rows.reshape(n_sec * capacity, comps * tile_len), precision=highest
    )
    counts = jnp.sum(slot_hot, axis=1)
    pulled = (
        pulled.reshape(sec_dev, rows_dev, per_row, comps, tile_len)
        .transpose(0, 3, 1, 2, 4)
        .reshape(sec_dev, comps, rows_dev, width)
    )
    counts = jnp.repeat(counts.reshape(sec_dev, rows_dev, per_row), tile_len, axis=2)
    stiffness = stiffness_map(classes, table)
    lower, diagonal, upper = band_coefs(z_couple)

    def forward_coef(previous, coefs):
        low_c, diag_c, up_c = coefs
        pivot = diag_c - low_c * previous
        ratio = up_c / pivot
        return (ratio, (ratio, pivot))

    ignored, (ratio_all, pivot_all) = lax.scan(
        forward_coef, jnp.zeros((), z_couple.dtype), (lower, diagonal, upper)
    )
    columns = rows_dev * width // n_sec
    field = node_flow
    for cycle in range(ROUNDS):
        moved = field.reshape(sec_dev, comps, n_sec, columns)
        piece = lax.all_to_all(moved, "sec", split_axis=2, concat_axis=0, tiled=True)
        sections = piece.shape[0]
        solved = lax.linalg.tridiagonal_solve(
            lower, diagonal, upper, piece.reshape(sections, -1)
        ).reshape(piece.shape)
        field = lax.all_to_all(solved, "sec", split_axis=0, concat_axis=2, tiled=True).reshape(
            sec_dev, comps, rows_dev, width
        )
        for step in range(ISTEPS):
            field = plane_step(field, stiffness, pulled, counts)
    return field


def solution(mesh):
    return jax.shard_map(
        local,
        mesh=mesh,
        in_specs=(
            P("sec", None, "tile", None),
            P("sec", "tile", None),
            P(),
            P(),
            P(("sec", "tile"), None),
            P(("sec", "tile")),
            P(("sec", "tile"), None),
        ),
        out_specs=P("sec", None, "tile", None),
        check_vma=False,
    )
```

profile of v0, /device:TPU:1, one launch (start us, length us, event | category | flops | bytes accessed | tf_op | source)
XLA Modules:
  0.0 1088.6 jit_solution(3961621274888284311)
XLA Ops:
  2.0 20.7 %all-to-all-start = ((f32[1,2,128,256]{3,1,0,2:T(2,128)}), f32[1,2,128,256]{3,1,0,2:T(2,128)S(1)}, u32[]{:S(2)}, u32[]{:S(2)}) async-start(f32[1,2,128,256]{3,1,0,2:T(2,128)} %copy.42), calls=%async_computation | async-start | bytes 524288 | tf_op jit(solution)/shard_map/all_to_all | solution.py:111
  31.9 13.2 %all-to-all-done = f32[1,2,128,256]{3,1,0,2:T(2,128)S(1)} async-done(((f32[1,2,128,256]{3,1,0,2:T(2,128)}), f32[1,2,128,256]{3,1,0,2:T(2,128)S(1)}, u32[]{:S(2)}, u32[]{:S(2)}) %all-to-all-start) | async-done | bytes 262176 | tf_op jit(solution)/shard_map/all_to_all | solution.py:111
  45.2 7.3 all-to-all-start.2
  53.4 253.2 %while.64 = (s32[]{:T(128)}, f32[]{:T(128)}, f32[512]{0:T(512)S(1)}, f32[3,32]{1,0:T(4,128)S(1)}, f32[3,32,512]{2,1,0:T(8,128)S(1)}, /*index=5*/f32[3,32]{1,0:T(...) while((s32[]{:T(128)}, f32[]{:T(128)}, ...), condition=%wide.region_1.2_spmd, body=%wide.region_0.0_spmd.sunk | while | flops 49281 | bytes 534781 | solution.py:113
  117.5 19.9 %subtract_divide_fusion.250 = (f32[512]{0:T(512)S(1)}, f32[512]{0:T(512)S(1)}, f32[512]{0:T(512)S(1)}, f32[512]{0:T(512)S(1)}, f32[512]{0:T(512)S(1)}, /*index=5...) fusion(f32[512]{0:T(512)S(1)} %bitcast.2665, ...), kind=kLoop, calls=%fused_computation.36.clone.1 | loop fusion | flops 49152 | bytes 133376 | tf_op jit(solution)/shard_map/while/body/eval_jaxpr/div | solution.py:113
  201.9 19.9 %subtract_divide_fusion.250 = (f32[512]{0:T(512)S(1)}, f32[512]{0:T(512)S(1)}, f32[512]{0:T(512)S(1)}, f32[512]{0:T(512)S(1)}, f32[512]{0:T(512)S(1)}, /*index=5...) fusion(f32[512]{0:T(512)S(1)} %bitcast.2665, ...), kind=kLoop, calls=%fused_computation.36.clone.1 | loop fusion | flops 49152 | bytes 133376 | tf_op jit(solution)/shard_map/while/body/eval_jaxpr/div | solution.py:113
  286.3 19.9 %subtract_divide_fusion.250 = (f32[512]{0:T(512)S(1)}, f32[512]{0:T(512)S(1)}, f32[512]{0:T(512)S(1)}, f32[512]{0:T(512)S(1)}, f32[512]{0:T(512)S(1)}, /*index=5...) fusion(f32[512]{0:T(512)S(1)} %bitcast.2665, ...), kind=kLoop, calls=%fused_computation.36.clone.1 | loop fusion | flops 49152 | bytes 133376 | tf_op jit(solution)/shard_map/while/body/eval_jaxpr/div | solution.py:113
  366.1 19.4 %subtract_divide_fusion.95 = (f32[512]{0:T(512)S(1)}, f32[512]{0:T(512)S(1)}, f32[512]{0:T(512)S(1)}, f32[512]{0:T(512)S(1)}, f32[512]{0:T(512)S(1)}, /*index=5*...) fusion(f32[512]{0:T(512)S(1)} %bitcast.2845, ...), kind=kLoop, calls=%fused_computation.555 | loop fusion | flops 47616 | bytes 129272 | tf_op jit(solution)/shard_map/eval_jaxpr/div | solution.py:113
  386.0 64.7 %while.65 = (s32[]{:T(128)}, f32[512]{0:T(512)S(1)}, f32[3,32,512]{2,1,0:T(8,128)S(1)}, f32[3,32,512]{2,1,0:T(8,128)S(1)}, f32[3,32]{1,0:T(4,128)S(1)}, /*index=...) while((s32[]{:T(128)}, f32[512]{0:T(512)S(1)}, ...), condition=%wide.region_3.4_spmd, body=%wide.region_2.3_spmd.sunk | while | flops 32802 | bytes 531937 | solution.py:113
  387.6 19.7 %multiply_subtract_fusion.250 = (f32[512]{0:T(512)S(1)}, f32[512]{0:T(512)S(1)}, f32[512]{0:T(512)S(1)}, f32[512]{0:T(512)S(1)}, f32[512]{0:T(512)S(1)}, /*index...) fusion(f32[512]{0:T(512)S(1)} %bitcast.2571, ...), kind=kLoop, calls=%fused_computation.102.clone.1 | loop fusion | flops 32768 | bytes 133248 | tf_op jit(solution)/shard_map/while/body/eval_jaxpr/sub | solution.py:113
  409.2 19.7 %multiply_subtract_fusion.250 = (f32[512]{0:T(512)S(1)}, f32[512]{0:T(512)S(1)}, f32[512]{0:T(512)S(1)}, f32[512]{0:T(512)S(1)}, f32[512]{0:T(512)S(1)}, /*index...) fusion(f32[512]{0:T(512)S(1)} %bitcast.2571, ...), kind=kLoop, calls=%fused_computation.102.clone.1 | loop fusion | flops 32768 | bytes 133248 | tf_op jit(solution)/shard_map/while/body/eval_jaxpr/sub | solution.py:113
  430.7 19.7 %multiply_subtract_fusion.250 = (f32[512]{0:T(512)S(1)}, f32[512]{0:T(512)S(1)}, f32[512]{0:T(512)S(1)}, f32[512]{0:T(512)S(1)}, f32[512]{0:T(512)S(1)}, /*index...) fusion(f32[512]{0:T(512)S(1)} %bitcast.2571, ...), kind=kLoop, calls=%fused_computation.102.clone.1 | loop fusion | flops 32768 | bytes 133248 | tf_op jit(solution)/shard_map/while/body/eval_jaxpr/sub | solution.py:113
  450.7 19.4 %multiply_subtract_fusion.95 = (f32[512]{0:T(512)S(1)}, f32[512]{0:T(512)S(1)}, f32[512]{0:T(512)S(1)}, f32[512]{0:T(512)S(1)}, f32[512]{0:T(512)S(1)}, /*index=...) fusion(f32[512]{0:T(512)S(1)} %bitcast.2824, ...), kind=kLoop, calls=%fused_computation.524 | loop fusion | flops 31744 | bytes 129148 | tf_op jit(solution)/shard_map/eval_jaxpr/sub | solution.py:113
  489.8 16.3 %all-to-all-start.1 = ((f32[128,2,1,256]{3,1,2,0:T(2,128)}), f32[128,2,1,256]{3,1,2,0:T(2,128)S(1)}, u32[]{:S(2)}, u32[]{:S(2)}) async-start(f32[128,2,1,256]{3,1,2,0:T(2,128)} %constant_dynamic-update-slice_fusion), calls=%async_computation.1 | async-start | bytes 524288 | tf_op jit(solution)/shard_map/all_to_all | solution.py:116
  507.5 21.1 %all-to-all-done.1 = f32[128,2,1,256]{3,1,2,0:T(2,128)S(1)} async-done(((f32[128,2,1,256]{3,1,2,0:T(2,128)}), f32[128,2,1,256]{3,1,2,0:T(2,128)S(1)}, u32[]{:S(2)}, u32[]{:S(2)}) %all-to-all-start.1) | async-done | bytes 262176 | tf_op jit(solution)/shard_map/all_to_all | solution.py:116
  528.6 7.4 all-to-all-start.3
  536.8 5.0 add_bitcast_fusion
  542.8 26.6 %all-to-all-done.3 = f32[128,4,256]{2,1,0:T(4,128)S(1)} async-done(((f32[128,4,256]{2,1,0:T(4,128)}), f32[128,4,256]{2,1,0:T(4,128)S(1)}, u32[]{:S(2)}, u32[]{:S(2)}) %all-to-all-start.3) | async-done | bytes 524320 | tf_op jit(solution)/shard_map/all_to_all | solution.py:78
  588.4 9.4 all-to-all-start.4
  597.9 22.5 %all-to-all-done.4 = f32[1,2,128,256]{3,1,0,2:T(2,128)S(1)} async-done(((f32[1,2,128,256]{3,1,0,2:T(2,128)}), f32[1,2,128,256]{3,1,0,2:T(2,128)S(1)}, u32[]{:S(2)}, u32[]{:S(2)}) %all-to-all-start.4) | async-done | bytes 262176 | tf_op jit(solution)/shard_map/all_to_all | solution.py:111
  621.3 253.9 %while.66 = (s32[]{:T(128)}, f32[]{:T(128)}, f32[512]{0:T(512)S(1)}, f32[3,32]{1,0:T(4,128)S(1)}, f32[3,32,512]{2,1,0:T(8,128)S(1)}, /*index=5*/f32[3,32]{1,0:T(...) while((s32[]{:T(128)}, f32[]{:T(128)}, ...), condition=%wide.region_9.10_spmd, body=%wide.region_8.9_spmd.sunk | while | flops 49281 | bytes 534781 | solution.py:113
  685.6 20.0 %subtract_divide_fusion.251 = (f32[512]{0:T(512)S(1)}, f32[512]{0:T(512)S(1)}, f32[512]{0:T(512)S(1)}, f32[512]{0:T(512)S(1)}, f32[512]{0:T(512)S(1)}, /*index=5...) fusion(f32[512]{0:T(512)S(1)} %bitcast.2679, ...), kind=kLoop, calls=%fused_computation.170.clone.1 | loop fusion | flops 49152 | bytes 133376 | tf_op jit(solution)/shard_map/while/body/eval_jaxpr/div | solution.py:113
  770.2 20.0 %subtract_divide_fusion.251 = (f32[512]{0:T(512)S(1)}, f32[512]{0:T(512)S(1)}, f32[512]{0:T(512)S(1)}, f32[512]{0:T(512)S(1)}, f32[512]{0:T(512)S(1)}, /*index=5...) fusion(f32[512]{0:T(512)S(1)} %bitcast.2679, ...), kind=kLoop, calls=%fused_computation.170.clone.1 | loop fusion | flops 49152 | bytes 133376 | tf_op jit(solution)/shard_map/while/body/eval_jaxpr/div | solution.py:113
  854.8 20.0 %subtract_divide_fusion.251 = (f32[512]{0:T(512)S(1)}, f32[512]{0:T(512)S(1)}, f32[512]{0:T(512)S(1)}, f32[512]{0:T(512)S(1)}, f32[512]{0:T(512)S(1)}, /*index=5...) fusion(f32[512]{0:T(512)S(1)} %bitcast.2679, ...), kind=kLoop, calls=%fused_computation.170.clone.1 | loop fusion | flops 49152 | bytes 133376 | tf_op jit(solution)/shard_map/while/body/eval_jaxpr/div | solution.py:113
  934.6 19.4 %subtract_divide_fusion.64 = (f32[512]{0:T(512)S(1)}, f32[512]{0:T(512)S(1)}, f32[512]{0:T(512)S(1)}, f32[512]{0:T(512)S(1)}, f32[512]{0:T(512)S(1)}, /*index=5*...) fusion(f32[512]{0:T(512)S(1)} %bitcast.2844, ...), kind=kLoop, calls=%fused_computation.492 | loop fusion | flops 47616 | bytes 129272 | tf_op jit(solution)/shard_map/eval_jaxpr/div | solution.py:113
  954.6 65.5 %while.67 = (s32[]{:T(128)}, f32[512]{0:T(512)S(1)}, f32[3,32,512]{2,1,0:T(8,128)S(1)}, f32[3,32,512]{2,1,0:T(8,128)S(1)}, f32[3,32]{1,0:T(4,128)S(1)}, /*index=...) while((s32[]{:T(128)}, f32[512]{0:T(512)S(1)}, ...), condition=%wide.region_11.12_spmd, body=%wide.region_10.11_spmd.sunk | while | flops 32802 | bytes 531937 | solution.py:113
  956.2 20.0 %multiply_subtract_fusion.251 = (f32[512]{0:T(512)S(1)}, f32[512]{0:T(512)S(1)}, f32[512]{0:T(512)S(1)}, f32[512]{0:T(512)S(1)}, f32[512]{0:T(512)S(1)}, /*index...) fusion(f32[512]{0:T(512)S(1)} %bitcast.2589, ...), kind=kLoop, calls=%fused_computation.236.clone.1 | loop fusion | flops 32768 | bytes 133248 | tf_op jit(solution)/shard_map/while/body/eval_jaxpr/sub | solution.py:113
  978.0 20.0 %multiply_subtract_fusion.251 = (f32[512]{0:T(512)S(1)}, f32[512]{0:T(512)S(1)}, f32[512]{0:T(512)S(1)}, f32[512]{0:T(512)S(1)}, f32[512]{0:T(512)S(1)}, /*index...) fusion(f32[512]{0:T(512)S(1)} %bitcast.2589, ...), kind=kLoop, calls=%fused_computation.236.clone.1 | loop fusion | flops 32768 | bytes 133248 | tf_op jit(solution)/shard_map/while/body/eval_jaxpr/sub | solution.py:113
  999.9 20.0 %multiply_subtract_fusion.251 = (f32[512]{0:T(512)S(1)}, f32[512]{0:T(512)S(1)}, f32[512]{0:T(512)S(1)}, f32[512]{0:T(512)S(1)}, f32[512]{0:T(512)S(1)}, /*index...) fusion(f32[512]{0:T(512)S(1)} %bitcast.2589, ...), kind=kLoop, calls=%fused_computation.236.clone.1 | loop fusion | flops 32768 | bytes 133248 | tf_op jit(solution)/shard_map/while/body/eval_jaxpr/sub | solution.py:113
  1020.1 19.4 %multiply_subtract_fusion.64 = (f32[512]{0:T(512)S(1)}, f32[512]{0:T(512)S(1)}, f32[512]{0:T(512)S(1)}, f32[512]{0:T(512)S(1)}, f32[512]{0:T(512)S(1)}, /*index=...) fusion(f32[512]{0:T(512)S(1)} %bitcast.2793, ...), kind=kLoop, calls=%fused_computation.461 | loop fusion | flops 31744 | bytes 129148 | tf_op jit(solution)/shard_map/eval_jaxpr/sub | solution.py:113
  1040.4 29.2 %all_to_all.74 = f32[128,2,1,256]{3,1,2,0:T(2,128)S(1)} all-to-all(f32[128,2,1,256]{3,1,2,0:T(2,128)S(1)} %constant_dynamic-update-slice_fusion.33), channel_id=1, replica_groups=mesh['sec'=128,'tile'=4] {'sec'}, dimensions={0} | all-to-all | bytes 524288 | tf_op jit(solution)/shard_map/all_to_all | solution.py:116
  1071.3 4.5 collective-permute-start.5
  (458 shorter events, 112.2 us)
Async XLA Ops:
  0.0 506.1 %copy-start = (f32[256,256]{1,0:T(8,128)S(1)}, f32[256,256]{1,0:T(8,128)}, u32[]{:S(2)}) copy-start(f32[256,256]{1,0:T(8,128)} %param.21) | copy-start | bytes 786436
  2.0 20.7 %copy-start.5 = (f32[128]{0:T(128)S(1)}, f32[128]{0:T(128)}, u32[]{:S(2)}) copy-start(f32[128]{0:T(128)} %param.18) | copy-start | bytes 1540
  2.0 43.2 %all-to-all-start = ((f32[1,2,128,256]{3,1,0,2:T(2,128)}), f32[1,2,128,256]{3,1,0,2:T(2,128)S(1)}, u32[]{:S(2)}, u32[]{:S(2)}) async-start(f32[1,2,128,256]{3,1,0,2:T(2,128)} %copy.42), calls=%async_computation | async-start | bytes 524288 | tf_op jit(solution)/shard_map/all_to_all | solution.py:111
  23.5 0.7 copy-start.3
  24.5 0.7 copy-start.4
  45.2 444.7 %all-to-all-start.2 = ((f32[128,1,4]{2,1,0:T(1,128)}), f32[128,1,4]{2,1,0:T(1,128)S(1)}, u32[]{:S(2)}, u32[]{:S(2)}) async-start(f32[128,1,4]{2,1,0:T(1,128)} %bitcast.823), calls=%async_computation.2 | async-start | bytes 131072 | tf_op jit(solution)/shard_map/all_to_all | solution.py:79
  489.8 38.8 %all-to-all-start.1 = ((f32[128,2,1,256]{3,1,2,0:T(2,128)}), f32[128,2,1,256]{3,1,2,0:T(2,128)S(1)}, u32[]{:S(2)}, u32[]{:S(2)}) async-start(f32[128,2,1,256]{3,1,2,0:T(2,128)} %constant_dynamic-update-slice_fusion), calls=%async_computation.1 | async-start | bytes 524288 | tf_op jit(solution)/shard_map/all_to_all | solution.py:116
  528.6 7.4 copy-start.2
  528.6 8.1 copy-start.1
  528.6 40.7 %all-to-all-start.3 = ((f32[128,4,256]{2,1,0:T(4,128)}), f32[128,4,256]{2,1,0:T(4,128)S(1)}, u32[]{:S(2)}, u32[]{:S(2)}) async-start(f32[128,4,256]{2,1,0:T(4,128)} %reshape.1271), calls=%async_computation.3 | async-start | bytes 1048576 | tf_op jit(solution)/shard_map/all_to_all | solution.py:78
  569.8 5.9 collective-permute-start
  571.1 4.7 collective-permute-start.1
  578.3 5.5 collective-permute-start.2
  579.6 5.0 collective-permute-start.3
  588.4 31.9 %all-to-all-start.4 = ((f32[1,2,128,256]{3,1,0,2:T(2,128)}), f32[1,2,128,256]{3,1,0,2:T(2,128)S(1)}, u32[]{:S(2)}, u32[]{:S(2)}) async-start(f32[1,2,128,256]{3,1,0,2:T(2,128)} %copy.49), calls=%async_computation.4 | async-start | bytes 524288 | tf_op jit(solution)/shard_map/all_to_all | solution.py:111
  1070.0 5.8 collective-permute-start.4
  1071.3 5.3 collective-permute-start.5
  1079.1 5.6 collective-permute-start.6
  1080.4 5.0 collective-permute-start.7
where the time goes:
time: 1110 us; the launch traced here: 1090 us
  loops' own time  359 us (32%)
  other arithmetic  334 us (30%)
  between operations  118 us (11%)
  waiting for transfers between devices  85.7 us (8%)
  starting transfers between devices  83.3 us (8%)
  local copies, waits for them, and re-layouts  78.5 us (7%)
  blocking collectives  29.2 us (3%)
    another operation x4, loops' own time, local(): lax.linalg.tridiagonal_solve(lower, diagonal, upper, piece.reshape(sectio...  359 us
    div x8, other arithmetic, local(): lax.linalg.tridiagonal_solve(lower, diagonal, upper, piece.reshape(sectio...  159 us
    sub x8, other arithmetic, local(): lax.linalg.tridiagonal_solve(lower, diagonal, upper, piece.reshape(sectio...  158 us
    slice x95, local copies, waits for them, and re-layouts, local(): lax.linalg.tridiagonal_solve(lower, diagonal, upper, piece.reshape(sectio...  44.2 us
    all_to_all x2, waiting for transfers between devices, local(): lax.all_to_all(moved, 'sec', split_axis=2, concat_axis=0, tiled=True)  35.7 us
    all_to_all x2, starting transfers between devices, local(): lax.all_to_all(moved, 'sec', split_axis=2, concat_axis=0, tiled=True)  30.1 us
    all_to_all x1, blocking collectives, local(): lax.all_to_all(solved, 'sec', split_axis=0, concat_axis=2, tiled=True)  29.2 us
    all_to_all x1, waiting for transfers between devices, local(): lax.all_to_all(send_rows, 'sec', split_axis=0, concat_axis=0, tiled=True)  26.6 us
  transfers between devices with their start and end apart: 13, of which 8 were waited for; matrix products, arithmetic and copies ran while one was open for 20% of the time, Pallas kernels for 0%

commit v1 on v0

v1 whole, which is shorter than its diff:
```python
import functools

import jax
import jax.numpy as jnp
from jax import lax
from jax.experimental import pallas as pl
from jax.experimental.pallas import tpu as pltpu
from jax.sharding import PartitionSpec as P

MESH = pl.DeviceIdType.MESH
RELAX = 0.05
CAP = 4
F32 = jnp.float32
BF16 = jnp.bfloat16


def iota(shape, dim):
    return lax.broadcasted_iota(jnp.int32, shape, dim)


def split3(v):
    hi = v.astype(BF16)
    rest = v - hi.astype(F32)
    mid = rest.astype(BF16)
    lo = (rest - mid.astype(F32)).astype(BF16)
    return hi, mid, lo


def inverse_parts(z, n):
    lanes = z.shape[1]
    lane = iota(z.shape, 1)
    w = 1.0 / z
    one = jnp.ones_like(z)
    m = (one, w, one, 1.0 + w)
    step = 1
    while step < n:
        first = lane < step
        b = [jnp.where(first, float(k in (0, 3)), pltpu.roll(v, step, 1)) for k, v in enumerate(m)]
        a = m
        m = (
            a[0] * b[0] + a[1] * b[2],
            a[0] * b[1] + a[1] * b[3],
            a[2] * b[0] + a[3] * b[2],
            a[2] * b[1] + a[3] * b[3],
        )
        step *= 2
    p_next = m[0] + m[1]
    p = jnp.where(lane == 0, 1.0, pltpu.roll(p_next, 1, 1))
    t = jnp.where(lane < n, 1.0 / (z * p * p_next), 0.0)
    p, t = p[:1], t[:1]
    r, c = iota((lanes, lanes), 0), iota((lanes, lanes), 1)
    p_col = jnp.sum(jnp.where(r == c, p, 0.0), axis=1, keepdims=True)
    t_col = jnp.sum(jnp.where(r == c, t, 0.0), axis=1, keepdims=True)
    tail_col = jnp.sum(jnp.where(c >= r, t, 0.0), axis=1, keepdims=True)
    tail = jnp.sum(jnp.where(r >= c, t_col, 0.0), axis=0, keepdims=True)
    return p, tail, p_col, tail_col


def kernel(
    dims,
    node_ref, classes_ref, table_ref, z_ref, dest_ref, slot_ref, vec_ref, out_ref,
    fin, xs, ext, fld, pq_send, pq_recv, lhs, cols,
    ma_send, ma_recv, mb_recv, sa_send, sa_recv, sb_send, sb_recv,
    halo_send, halo_recv, coef, cls, vec,
    load_sem, fin_send_sem, fin_recv_sem, pq_send_sem, pq_recv_sem, out_send_sem, out_recv_sem,
    ma_send_sem, ma_recv_sem, sa_send_sem, sa_recv_sem,
    mb_send_sem, mb_recv_sem, sb_send_sem, sb_recv_sem, halo_send_sem, halo_recv_sem,
):
    n_y, line, n_tile, rows, width = dims
    n_sec = n_y * line
    per_row = width // 128
    sec, t = lax.axis_index("sec"), lax.axis_index("tile")
    y, i = sec // line, sec % line
    tops = rows // 8

    def at_line(j):
        return (y * line + j, t)

    def at_y(q):
        return (q * line + i, t)

    def at_tile(s):
        return (sec, s)

    before, after = (t + n_tile - 1) % n_tile, (t + 1) % n_tile

    loads = [
        pltpu.make_async_copy(vec_ref, vec, load_sem.at[0]),
        pltpu.make_async_copy(classes_ref.at[0], cls, load_sem.at[1]),
    ]
    for load in loads:
        load.start()
    barrier = pltpu.get_barrier_semaphore()

    @pl.loop(1, line)
    def _(k):
        pl.semaphore_signal(barrier, inc=1, device_id=at_line((i + k) % line), device_id_type=MESH)

    for k in range(1, n_y):
        pl.semaphore_signal(barrier, inc=1, device_id=at_y((y + k) % n_y), device_id_type=MESH)
    for s in (before, after):
        pl.semaphore_signal(barrier, inc=1, device_id=at_tile(s), device_id_type=MESH)

    for r in range(2):
        ext[r, :, 0:8, :] = jnp.zeros((2, 8, width), F32)
        ext[r, :, rows + 8 :, :] = jnp.zeros((2, 8, width), F32)
    coef[:, 0:8, :] = jnp.zeros((4, 8, width), F32)
    coef[:, rows + 8 :, :] = jnp.zeros((4, 8, width), F32)

    pl.semaphore_wait(barrier, line - 1 + n_y - 1 + 2)

    def piece(field, j, base):
        top = pl.multiple_of(base + (j // per_row) * 8, 8)
        left = pl.multiple_of((j % per_row) * 128, 128)
        return field.at[:, pl.ds(top, 8), pl.ds(left, 128)]

    def send_in(field, r):
        pltpu.make_async_copy(piece(field, i, 0), fin.at[r, i], fin_recv_sem.at[r]).start()

        @pl.loop(1, line)
        def _(k):
            j = (i + k) % line
            pltpu.make_async_remote_copy(
                src_ref=piece(field, j, 0), dst_ref=fin.at[r, i],
                send_sem=fin_send_sem.at[r], recv_sem=fin_recv_sem.at[r],
                device_id=at_line(j), device_id_type=MESH,
            ).start()

    def wait_for(ref, sem):
        pltpu.make_async_copy(ref, ref, sem).wait()

    send_in(node_ref.at[0], 0)

    dest, slot = dest_ref[...], slot_ref[...]
    matches = dest.shape[1]
    hot = (iota((n_sec, matches), 0) == dest).astype(F32)
    earlier = (iota((matches, matches), 0) < iota((matches, matches), 1)).astype(BF16)
    hits = jnp.dot(hot.astype(BF16), earlier, preferred_element_type=F32)
    rank = jnp.sum(hot * hits, axis=0, keepdims=True).astype(jnp.int32)
    spot = (slot % per_row) * rows + slot // per_row
    base = 8 * n_y * (i % 4) + 8 * y + rank
    lane = iota((128, matches), 0)
    marks = jnp.where((lane == base) | (lane == base + CAP), (spot + 1).astype(F32), 0.0)
    sa_send[...] = lax.dot_general(
        hot.astype(BF16), marks.astype(BF16), (((1,), (1,)), ((), ())), preferred_element_type=F32
    ).reshape(n_y, line, 128)
    position = dest * 8 + rank
    position = jnp.concatenate([position, position + CAP], axis=1)
    loads[0].wait()
    vectors = vec[...]
    vectors = jnp.concatenate([vectors[:, :128], vectors[:, 128:]], axis=0)
    vectors = jnp.concatenate(split3(vectors), axis=1)
    for k in range(n_y):
        q = (y + k) % n_y
        place = (iota((line * 8, 2 * matches), 0) + q * (line * 8) == position).astype(F32).astype(BF16)
        packed = jnp.dot(place, vectors, preferred_element_type=F32)
        packed = (packed[:, :128] + packed[:, 128:256]) + packed[:, 256:]
        ma_send[q] = packed.reshape(line, 8, 128)
        if k == 0:
            pltpu.make_async_copy(ma_send.at[q], ma_recv.at[:, y], ma_recv_sem).start()
            pltpu.make_async_copy(sa_send.at[q], sa_recv.at[y], sa_recv_sem).start()
        else:
            pltpu.make_async_remote_copy(
                src_ref=ma_send.at[q], dst_ref=ma_recv.at[:, y], send_sem=ma_send_sem, recv_sem=ma_recv_sem,
                device_id=at_y(q), device_id_type=MESH,
            ).start()
            pltpu.make_async_remote_copy(
                src_ref=sa_send.at[q], dst_ref=sa_recv.at[y], send_sem=sa_send_sem, recv_sem=sa_recv_sem,
                device_id=at_y(q), device_id_type=MESH,
            ).start()

    z = jnp.broadcast_to(z_ref[...], (8, 128))
    p, tail, p_col, tail_col = inverse_parts(z, n_sec)
    full = p_col * (p * jnp.minimum(tail_col, tail))
    pt, pt_col = p * tail, p_col * tail_col
    block, p_own, pt_own = jnp.zeros((line, line), F32), jnp.zeros((1, line), F32), jnp.zeros((1, line), F32)
    p_own_col, pt_own_col = jnp.zeros((line, 1), F32), jnp.zeros((line, 1), F32)
    for q in range(n_y):
        here, cut = y == q, slice(q * line, (q + 1) * line)
        block = jnp.where(here, full[cut, cut], block)
        p_own, pt_own = jnp.where(here, p[:, cut], p_own), jnp.where(here, pt[:, cut], pt_own)
        p_own_col = jnp.where(here, p_col[cut], p_own_col)
        pt_own_col = jnp.where(here, pt_col[cut], pt_own_col)
    lhs[0:line, :] = block
    lhs[line : line + 8, :] = jnp.concatenate([p_own, pt_own, jnp.zeros((6, line), F32)], axis=0)
    cols[0] = jnp.broadcast_to(p_own_col, (line, 128))
    cols[1] = jnp.broadcast_to(pt_own_col, (line, 128))

    loads[1].wait()
    classes = cls[...]
    stiffness = jnp.zeros((rows, width), F32)
    for level in range(table_ref.shape[0]):
        stiffness = jnp.where(classes == level, table_ref[level], stiffness)
    coef[0, 8 : rows + 8, :] = RELAX * stiffness

    def forward_matches():
        wait_for(ma_recv, ma_recv_sem)
        wait_for(sa_recv, sa_recv_sem)
        marked = jnp.sum(sa_recv[...], axis=0)
        for j in range(line):
            sb_send[j] = marked[j : j + 1]
        pltpu.make_async_copy(sb_send.at[i], sb_recv.at[i], sb_recv_sem).start()
        pltpu.make_async_copy(ma_recv.at[i], mb_recv.at[i], mb_recv_sem).start()

        @pl.loop(1, line)
        def _(k):
            j = (i + k) % line
            pltpu.make_async_remote_copy(
                src_ref=sb_send.at[j], dst_ref=sb_recv.at[i], send_sem=sb_send_sem, recv_sem=sb_recv_sem,
                device_id=at_line(j), device_id_type=MESH,
            ).start()
            pltpu.make_async_remote_copy(
                src_ref=ma_recv.at[j], dst_ref=mb_recv.at[i], send_sem=mb_send_sem, recv_sem=mb_recv_sem,
                device_id=at_line(j), device_id_type=MESH,
            ).start()

    def place_matches():
        wait_for(sb_recv, sb_recv_sem)
        wait_for(mb_recv, mb_recv_sem)
        total = line * n_y * 8
        chunks = []
        for g in range(line // 4):
            chunks.append(jnp.sum(jnp.sum(sb_recv[4 * g : 4 * g + 4], axis=0), axis=0, keepdims=True)[:, : 32 * n_y])
        ids = jnp.concatenate(chunks, axis=1).astype(jnp.int32)
        comp = (iota((1, total), 1) // CAP) % 2
        rhs = mb_recv[...].reshape(total, 128)
        rhs = jnp.concatenate([*split3(rhs), jnp.ones((total, 128), BF16)], axis=1)
        spots = rows * per_row
        for c in range(2):
            target = jnp.where(comp == c, ids - 1, -1)
            chosen = (iota((spots, total), 0) == target).astype(F32).astype(BF16)
            sums = jnp.dot(chosen, rhs, preferred_element_type=F32)
            pulled = (sums[:, :128] + sums[:, 128:256]) + sums[:, 256:384]
            for b in range(per_row):
                cut = slice(b * rows, (b + 1) * rows)
                lanes = slice(b * 128, (b + 1) * 128)
                coef[2 + c, 8 : rows + 8, lanes] = RELAX * pulled[cut]
                if c == 0:
                    coef[1, 8 : rows + 8, lanes] = (
                        1.0 - 4.0 * coef[0, 8 : rows + 8, lanes] - RELAX * sums[cut, 384:]
                    )

    def solve(r):
        wait_for(fin.at[r], fin_recv_sem.at[r])
        f = jnp.concatenate([fin[r, :, c, s, :] for c in range(2) for s in range(8)], axis=1)
        got = jnp.dot(lhs[...], f, precision=lax.Precision.HIGHEST, preferred_element_type=F32)
        pq_send[r] = got[line : line + 2]
        pltpu.make_async_copy(pq_send.at[r], pq_recv.at[r, y], pq_recv_sem.at[r]).start()
        for k in range(1, n_y):
            pltpu.make_async_remote_copy(
                src_ref=pq_send.at[r], dst_ref=pq_recv.at[r, y], send_sem=pq_send_sem.at[r],
                recv_sem=pq_recv_sem.at[r], device_id=at_y((y + k) % n_y), device_id_type=MESH,
            ).start()
        if r == 0:
            forward_matches()
        wait_for(pq_recv.at[r], pq_recv_sem.at[r])
        below, above = jnp.zeros((1, 2048), F32), jnp.zeros((1, 2048), F32)
        for q in range(n_y):
            pair = pq_recv[r, q]
            below = below + jnp.where(q < y, pair[0:1], 0.0)
            above = above + jnp.where(q > y, pair[1:2], 0.0)
        for c in range(2):
            for s in range(8):
                cut = slice((c * 8 + s) * 128, (c * 8 + s + 1) * 128)
                xs[r, :, c, s, :] = got[0:line, cut] + cols[1] * below[:, cut] + cols[0] * above[:, cut]
        pltpu.make_async_copy(xs.at[r, i], piece(ext.at[r], i, 8), out_recv_sem.at[r]).start()

        @pl.loop(1, line)
        def _(k):
            j = (i + k) % line
            pltpu.make_async_remote_copy(
                src_ref=xs.at[r, j], dst_ref=piece(ext.at[r], i, 8),
                send_sem=out_send_sem.at[r], recv_sem=out_recv_sem.at[r],
                device_id=at_line(j), device_id_type=MESH,
            ).start()

    def halo(r):
        top = [ext[r, c, 8:10, :] for c in range(2)] + [coef[k, 8:9, :] for k in range(4)]
        last = rows + 8
        low = [ext[r, c, last - 2 : last, :] for c in range(2)] + [coef[k, last - 1 : last, :] for k in range(4)]
        halo_send[r, 0] = jnp.concatenate(top, axis=0)
        halo_send[r, 1] = jnp.concatenate(low, axis=0)
        for side, other in ((0, before), (1, after)):
            pltpu.make_async_remote_copy(
                src_ref=halo_send.at[r, side], dst_ref=halo_recv.at[r, side], send_sem=halo_send_sem.at[r],
                recv_sem=halo_recv_sem.at[r], device_id=at_tile(other), device_id_type=MESH,
            ).start()
        wait_for(halo_recv.at[r], halo_recv_sem.at[r])
        above = jnp.where(t > 0, halo_recv[r, 1], 0.0)
        below = jnp.where(t < n_tile - 1, halo_recv[r, 0], 0.0)
        for c in range(2):
            ext[r, c, 6:8, :] = above[2 * c : 2 * c + 2]
            ext[r, c, last : last + 2, :] = below[2 * c : 2 * c + 2]
        if r == 0:
            for k in range(4):
                coef[k, 7:8, :] = above[4 + k : 5 + k]
                coef[k, last : last + 1, :] = below[4 + k : 5 + k]

    def relax(r, store):
        height = rows + 16
        column = iota((height, width), 1)
        a, e = coef[0], coef[1]
        for c in range(2):
            v = ext[r, c]
            for _ in range(2):
                left = jnp.where(column == 0, 0.0, pltpu.roll(v, 1, 1))
                right = jnp.where(column == width - 1, 0.0, pltpu.roll(v, width - 1, 1))
                around = (pltpu.roll(v, 1, 0) + pltpu.roll(v, height - 1, 0)) + (left + right)
                v = e * v + (a * around + coef[2 + c])
            store(c, v[8 : rows + 8])

    def keep(c, v):
        fld[c] = v

    def finish(c, v):
        out_ref[0, c] = v

    for r in range(2):
        solve(r)
        if r == 0:
            place_matches()
        wait_for(ext.at[r, :, pl.ds(8, rows)], out_recv_sem.at[r])
        halo(r)
        if r == 0:
            relax(r, keep)
            send_in(fld, 1)
        else:
            relax(r, finish)

    for r in range(2):
        wait_for(fin.at[r, pl.ds(0, line - 1)], fin_send_sem.at[r])
        wait_for(xs.at[r, pl.ds(0, line - 1)], out_send_sem.at[r])
        wait_for(pq_recv.at[r, pl.ds(0, n_y - 1)], pq_send_sem.at[r])
        wait_for(halo_send.at[r], halo_send_sem.at[r])
    wait_for(ma_send.at[pl.ds(0, n_y - 1)], ma_send_sem)
    wait_for(sa_send.at[pl.ds(0, n_y - 1)], sa_send_sem)
    wait_for(mb_recv.at[pl.ds(0, line - 1)], mb_send_sem)
    wait_for(sb_recv.at[pl.ds(0, line - 1)], sb_send_sem)


def local(n_sec, n_tile, node_flow, classes, table, z_couple, match_dest, match_slot, match_vectors):
    _, comps, rows, width = node_flow.shape
    line = rows * width // 1024
    n_y = n_sec // line
    matches = match_vectors.shape[0]
    vmem, dma = pltpu.VMEM, pltpu.SemaphoreType.DMA
    z = jnp.pad(z_couple, (0, 128 - n_sec), constant_values=26.0).reshape(1, 128)
    return pl.pallas_call(
        functools.partial(kernel, (n_y, line, n_tile, rows, width)),
        out_shape=jax.ShapeDtypeStruct(node_flow.shape, F32),
        in_specs=[
            pl.BlockSpec(memory_space=pl.ANY),
            pl.BlockSpec(memory_space=pl.ANY),
            pl.BlockSpec(memory_space=pltpu.SMEM),
            pl.BlockSpec(memory_space=vmem),
            pl.BlockSpec(memory_space=vmem),
            pl.BlockSpec(memory_space=vmem),
            pl.BlockSpec(memory_space=pl.ANY),
        ],
        out_specs=pl.BlockSpec(memory_space=vmem),
        scratch_shapes=[
            vmem((2, line, 2, 8, 128), F32),
            vmem((2, line, 2, 8, 128), F32),
            vmem((2, 2, rows + 16, width), F32),
            vmem((2, rows, width), F32),
            vmem((2, 2, 2048), F32),
            vmem((2, n_y, 2, 2048), F32),
            vmem((line + 8, line), F32),
            vmem((2, line, 128), F32),
            vmem((n_y, line, 8, 128), F32),
            vmem((line, n_y, 8, 128), F32),
            vmem((line, n_y, 8, 128), F32),
            vmem((n_y, line, 128), F32),
            vmem((n_y, line, 128), F32),
            vmem((line, 1, 128), F32),
            vmem((line, 1, 128), F32),
            vmem((2, 2, 8, width), F32),
            vmem((2, 2, 8, width), F32),
            vmem((4, rows + 16, width), F32),
            vmem((rows, width), jnp.int32),
            vmem((matches, 256), F32),
            dma((2,)),
            *([dma((2,))] * 6),
            *([dma(())] * 8),
            *([dma((2,))] * 2),
        ],
        compiler_params=pltpu.CompilerParams(
            collective_id=0, has_side_effects=True, vmem_limit_bytes=48 * 1024 * 1024
        ),
        cost_estimate=pl.CostEstimate(flops=2 * 10**9, bytes_accessed=10**6, transcendentals=0),
        name="align",
    )(
        node_flow,
        classes,
        table,
        z,
        match_dest.reshape(1, matches),
        match_slot.reshape(1, matches),
        match_vectors,
    )


def solution(mesh):
    return jax.shard_map(
        functools.partial(local, mesh.shape["sec"], mesh.shape["tile"]),
        mesh=mesh,
        in_specs=(
            P("sec", None, "tile", None),
            P("sec", "tile", None),
            P(),
            P(),
            P(("sec", "tile"), None),
            P(("sec", "tile")),
            P(("sec", "tile"), None),
        ),
        out_specs=P("sec", None, "tile", None),
        check_vma=False,
    )
```

time: 1110 us -> 118 us (0.11); the launches traced: 1090 us -> 118 us
  loops' own time: 359 us -> 0 us
  other arithmetic: 334 us -> 0 us
  between operations: 118 us -> 0.03 us
  Pallas kernels: 0 us -> 114 us
  waiting for transfers between devices: 85.7 us -> 0 us
  starting transfers between devices: 83.3 us -> 0 us
  local copies, waits for them, and re-layouts: 78.5 us -> 4.21 us
  blocking collectives: 29.2 us -> 0 us
    another operation x4 -> x0, loops' own time: 359 us -> none  [local(): lax.linalg.tridiagonal_solve(lower, diagonal, upper, piece.reshape(sectio...]
    div x8 -> x0, other arithmetic: 159 us -> none  [local(): lax.linalg.tridiagonal_solve(lower, diagonal, upper, piece.reshape(sectio...]
    sub x9 -> x0, other arithmetic: 158 us -> none  [the longest x8 158 us: local(): lax.linalg.tridiagonal_solve(lower, diagonal, upper, piece.reshape(sectio...]
    pallas_call x0 -> x1, Pallas kernels: none -> 114 us  [local(): pl.pallas_call(functools.partial(kernel, (n_y, line, n_tile, rows, width)...]
    all_to_all x5 -> x0, waiting for transfers between devices: 83.4 us -> none  [the longest x2 35.7 us: local(): lax.all_to_all(moved, 'sec', split_axis=2, concat_axis=0, tiled=True)]
    all_to_all x5 -> x0, starting transfers between devices: 61.1 us -> none  [the longest x2 30.1 us: local(): lax.all_to_all(moved, 'sec', split_axis=2, concat_axis=0, tiled=True)]
    slice x100 -> x0, local copies, waits for them, and re-layouts: 44.9 us -> none  [the longest x95 44.2 us: local(): lax.linalg.tridiagonal_solve(lower, diagonal, upper, piece.reshape(sectio...]
    all_to_all x1 -> x0, blocking collectives: 29.2 us -> none  [local(): lax.all_to_all(solved, 'sec', split_axis=0, concat_axis=2, tiled=True)]
  transfers between devices with their start and end apart: 13 -> 0, of which waited for: 8 -> 0; matrix products, arithmetic and copies ran while one was open for 20% -> 0% of each run, Pallas kernels for 0% -> 0%
where the time goes in v1:
time: 118 us
  Pallas kernels  114 us (97%)
  local copies, waits for them, and re-layouts  4.21 us (4%)
    pallas_call x1, Pallas kernels, local(): pl.pallas_call(functools.partial(kernel, (n_y, line, n_tile, rows, width)...  114 us
    unnamed x15, local copies, waits for them, and re-layouts  4.21 us

profile of v1, /device:TPU:1, one launch (start us, length us, event | category | flops | bytes accessed | tf_op | source)
XLA Modules:
  0.0 118.0 jit_solution(2636393851674097478)
XLA Ops:
  0.0 0.0 copy-start.4
  0.0 0.0 copy-start.6
  0.0 0.0 copy-start.3
  0.0 0.0 copy-start.5
  0.0 0.7 copy-done.4
  0.7 0.0 copy-done.6
  0.7 0.0 copy-done.3
  0.7 0.0 copy-done.5
  0.7 0.0 copy-start
  0.7 0.9 copy-done
  1.7 0.0 copy-start.1
  1.7 0.9 copy-done.1
  2.6 0.0 copy-start.2
  2.6 0.9 copy-done.2
  3.5 113.7 %align.1 = f32[1,2,64,512]{3,2,1,0:T(8,128)S(1)} custom-call(f32[1,2,64,512]{3,2,1,0:T(8,128)S(1)} %copy-done, s32[1,64,512]{2,1,0:T(8,128)S(1)} %copy-done.2, f32[8]{0:T(128)S(1)} %copy-done.5, f32[1,128]{1,0:T(1,128)S(1)} %bitcast.5, s32[1,256]{1,0:T(1,128)S(1)} %bitcast.3, s32[1,256]{1,0:T(1,128)S(1)} %bitcast.4, f32[256,256]{1,0:T(8,128)S(1)} %copy-done.1), custom_call_target="tpu_custom_call" | custom-call | flops 2000000000 | bytes 1000000 | tf_op jit(solution)/shard_map/align/pallas_call | solution.py:348
  117.3 0.7 copy.9
Async XLA Ops:
  0.0 0.7 copy-start.4
  0.0 0.7 copy-start.6
  0.0 0.7 copy-start.3
  0.0 0.7 copy-start.5
  0.7 1.0 copy-start
  1.7 0.9 copy-start.1
  2.6 0.9 copy-start.2

commit v2 on v1

v2 whole, which is shorter than its diff:
```python
import functools

import jax
import jax.numpy as jnp
from jax import lax
from jax.experimental import pallas as pl
from jax.experimental.pallas import tpu as pltpu
from jax.sharding import PartitionSpec as P

MESH = pl.DeviceIdType.MESH
RELAX = 0.05
CAP = 4
VMEM_LIMIT = 60 * 1024 * 1024
F32 = jnp.float32
BF16 = jnp.bfloat16


def iota(shape, dim):
    return lax.broadcasted_iota(jnp.int32, shape, dim)


def split3(v):
    hi = v.astype(BF16)
    rest = v - hi.astype(F32)
    mid = rest.astype(BF16)
    lo = (rest - mid.astype(F32)).astype(BF16)
    return hi, mid, lo


def inverse_parts(z, n):
    lanes = z.shape[1]
    lane = iota(z.shape, 1)
    w = 1.0 / z
    one = jnp.ones_like(z)
    m = (one, w, one, 1.0 + w)
    step = 1
    while step < n:
        first = lane < step
        b = [jnp.where(first, float(k in (0, 3)), pltpu.roll(v, step, 1)) for k, v in enumerate(m)]
        a = m
        m = (
            a[0] * b[0] + a[1] * b[2],
            a[0] * b[1] + a[1] * b[3],
            a[2] * b[0] + a[3] * b[2],
            a[2] * b[1] + a[3] * b[3],
        )
        step *= 2
    p_next = m[0] + m[1]
    p = jnp.where(lane == 0, 1.0, pltpu.roll(p_next, 1, 1))
    t = jnp.where(lane < n, 1.0 / (z * p * p_next), 0.0)
    p, t = p[:1], t[:1]
    r, c = iota((lanes, lanes), 0), iota((lanes, lanes), 1)
    p_col = jnp.sum(jnp.where(r == c, p, 0.0), axis=1, keepdims=True)
    tail_col = jnp.sum(jnp.where(c >= r, t, 0.0), axis=1, keepdims=True)
    return p_col, tail_col


def kernel(
    dims,
    node_ref, classes_ref, table_ref, z_ref, dest_ref, slot_ref, vec_ref, out_ref,
    fin, xs, ext, fld, pq_send, pq_recv, cols,
    ma_send, ma_recv, mb_recv, sa_send, sa_recv, sb_send, sb_recv,
    halo_send, halo_recv, coef, cls, vec, z_own, dest_own, slot_own, table,
    load_sem, fin_send_sem, fin_recv_sem, pq_send_sem, pq_recv_sem, out_send_sem, out_recv_sem,
    halo_send_sem, halo_recv_sem, ma_send_sem, ma_recv_sem, mb_send_sem, mb_recv_sem,
    sa_send_sem, sa_recv_sem, sb_send_sem, sb_recv_sem, store_sem,
):
    n_y, line, n_tile, rows, width = dims
    n_sec = n_y * line
    per_row = width // 128
    last = rows + 8
    sec, t = lax.axis_index("sec"), lax.axis_index("tile")
    y, i = sec // line, sec % line

    def at_line(j):
        return (y * line + j, t)

    def at_y(q):
        return (q * line + i, t)

    def at_tile(s):
        return (sec, s)

    def each_on_line(act):
        half = line // 2
        act((i + half) % line)

        @pl.loop(1, half)
        def _(k):
            act((i + half + k) % line)
            act((i + half - k) % line)

    def send(src, dst, send_sem, recv_sem, device):
        pltpu.make_async_remote_copy(
            src_ref=src, dst_ref=dst, send_sem=send_sem, recv_sem=recv_sem, device_id=device, device_id_type=MESH
        ).start()

    def keep(src, dst, sem):
        pltpu.make_async_copy(src, dst, sem).start()

    def wait_for(ref, sem):
        pltpu.make_async_copy(ref, ref, sem).wait()

    before, after = (t + n_tile - 1) % n_tile, (t + 1) % n_tile

    loads = [
        pltpu.make_async_copy(src, dst, load_sem.at[k])
        for k, (src, dst) in enumerate(
            (
                (dest_ref, dest_own),
                (slot_ref, slot_own),
                (vec_ref, vec),
                (z_ref, z_own),
                (table_ref, table),
                (classes_ref.at[0], cls),
            )
        )
    ]
    for load in loads:
        load.start()
    barrier = pltpu.get_barrier_semaphore()

    def greet(device):
        pl.semaphore_signal(barrier, inc=1, device_id=device, device_id_type=MESH)

    each_on_line(lambda j: greet(at_line(j)))
    for k in range(1, n_y):
        greet(at_y((y + k) % n_y))
    for s in (before, after):
        greet(at_tile(s))

    ext[:, :, 0:8, :] = jnp.zeros((2, 2, 8, width), F32)
    ext[:, :, last:, :] = jnp.zeros((2, 2, 8, width), F32)
    coef[:, 0:8, :] = jnp.zeros((4, 8, width), F32)
    coef[:, last:, :] = jnp.zeros((4, 8, width), F32)

    pl.semaphore_wait(barrier, line - 1 + n_y - 1 + 2)

    def piece(field, j, base):
        top = pl.multiple_of(base + (j // per_row) * 8, 8)
        left = pl.multiple_of((j % per_row) * 128, 128)
        return field.at[pl.ds(top, 8), pl.ds(left, 128)]

    def send_in(field, r, c):
        sems = fin_send_sem.at[r, c], fin_recv_sem.at[r, c]
        each_on_line(lambda j: send(piece(field, j, 0), fin.at[r, c, i], *sems, at_line(j)))
        keep(piece(field, i, 0), fin.at[r, c, i], sems[1])

    for c in range(2):
        send_in(node_ref.at[0, c], 0, c)

    loads[0].wait()
    loads[1].wait()
    dest, slot = dest_own[...], slot_own[...]
    matches = dest.shape[1]
    hot = (iota((n_sec, matches), 0) == dest).astype(F32)
    earlier = (iota((matches, matches), 0) < iota((matches, matches), 1)).astype(F32).astype(BF16)
    hits = jnp.dot(hot.astype(BF16), earlier, preferred_element_type=F32)
    rank = jnp.sum(hot * hits, axis=0, keepdims=True).astype(jnp.int32)
    spot = (slot % per_row) * rows + slot // per_row
    group = 128 // (CAP * n_y)
    base = CAP * n_y * (i % group) + CAP * y + rank
    marks = jnp.where(iota((128, matches), 0) == base, (spot + 1).astype(F32), 0.0)
    sa_send[...] = lax.dot_general(
        hot.astype(BF16), marks.astype(BF16), (((1,), (1,)), ((), ())), preferred_element_type=F32
    ).reshape(n_y, line, 128)
    position = dest * CAP + rank
    loads[2].wait()
    vectors = jnp.concatenate(split3(vec[...]), axis=1)
    for k in range(n_y):
        q = (y + k) % n_y
        place = (iota((line * CAP, matches), 0) + q * (line * CAP) == position).astype(F32).astype(BF16)
        packed = jnp.dot(place, vectors, preferred_element_type=F32)
        packed = (packed[:, :256] + packed[:, 256:512]) + packed[:, 512:]
        for c in range(2):
            ma_send[c, q] = packed[:, c * 128 : c * 128 + 128].reshape(line, CAP, 128)
            if k == 0:
                keep(ma_send.at[c, q], ma_recv.at[c, y], ma_recv_sem.at[c])
            else:
                send(ma_send.at[c, q], ma_recv.at[c, y], ma_send_sem.at[c], ma_recv_sem.at[c], at_y(q))
        if k == 0:
            keep(sa_send.at[q], sa_recv.at[y], sa_recv_sem)
        else:
            send(sa_send.at[q], sa_recv.at[y], sa_send_sem, sa_recv_sem, at_y(q))

    loads[3].wait()
    p_col, tail_col = inverse_parts(jnp.broadcast_to(z_own[...], (8, 128)), n_sec)
    pt_col = p_col * tail_col
    p_own, pt_own = p_col[:line], pt_col[:line]
    for q in range(1, n_y):
        cut = slice(q * line, (q + 1) * line)
        p_own, pt_own = jnp.where(y == q, p_col[cut], p_own), jnp.where(y == q, pt_col[cut], pt_own)
    cols[0] = jnp.broadcast_to(p_own, (line, 128))
    cols[1] = jnp.broadcast_to(pt_own, (line, 128))

    loads[4].wait()
    loads[5].wait()
    classes = cls[...]
    stiffness = jnp.zeros((rows, width), F32)
    for level in range(table.shape[0]):
        stiffness = jnp.where(classes == level, table[level], stiffness)
    coef[0, 8:last, :] = RELAX * stiffness

    def forward_slots():
        wait_for(sa_recv, sa_recv_sem)
        marked = jnp.sum(sa_recv[...], axis=0)
        for j in range(line):
            sb_send[j] = marked[j : j + 1]
        each_on_line(lambda j: send(sb_send.at[j], sb_recv.at[i], sb_send_sem, sb_recv_sem, at_line(j)))
        keep(sb_send.at[i], sb_recv.at[i], sb_recv_sem)

    def forward_matches(c):
        wait_for(ma_recv.at[c], ma_recv_sem.at[c])
        each_on_line(
            lambda j: send(ma_recv.at[c, :, j], mb_recv.at[c, i], mb_send_sem.at[c], mb_recv_sem.at[c], at_line(j))
        )
        keep(ma_recv.at[c, :, i], mb_recv.at[c, i], mb_recv_sem.at[c])

    spots, total = rows * per_row, line * n_y * CAP

    def choose():
        wait_for(sb_recv, sb_recv_sem)
        used = min(group, line)
        chunks = []
        for g in range(line // used):
            part = jnp.sum(jnp.sum(sb_recv[used * g : used * (g + 1)], axis=0), axis=0, keepdims=True)
            chunks.append(part[:, : used * n_y * CAP])
        ids = jnp.concatenate(chunks, axis=1).astype(jnp.int32) - 1
        chosen = (iota((spots, total), 0) == ids).astype(F32)
        counts = jnp.broadcast_to(jnp.sum(chosen, axis=1, keepdims=True), (spots, 128))
        for b in range(per_row):
            lanes = slice(b * 128, (b + 1) * 128)
            coef[1, 8:last, lanes] = (
                1.0 - 4.0 * coef[0, 8:last, lanes] - RELAX * counts[b * rows : (b + 1) * rows]
            )
        return chosen.astype(BF16)

    def place_matches(c, chosen):
        wait_for(mb_recv.at[c], mb_recv_sem.at[c])
        rhs = jnp.concatenate(split3(mb_recv[c].reshape(total, 128)), axis=1)
        sums = jnp.dot(chosen, rhs, preferred_element_type=F32)
        pulled = RELAX * ((sums[:, :128] + sums[:, 128:256]) + sums[:, 256:])
        for b in range(per_row):
            coef[2 + c, 8:last, b * 128 : (b + 1) * 128] = pulled[b * rows : (b + 1) * rows]

    def totals(r, c):
        wait_for(fin.at[r, c], fin_recv_sem.at[r, c])
        low, high = jnp.zeros((8, 128), F32), jnp.zeros((8, 128), F32)
        for j in range(line):
            f = fin[r, c, j]
            low, high = low + cols[0, j : j + 1] * f, high + cols[1, j : j + 1] * f
        pq_send[r, c, 0], pq_send[r, c, 1] = low, high
        sems = pq_send_sem.at[r, c], pq_recv_sem.at[r, c]
        for k in range(1, n_y):
            send(pq_send.at[r, c], pq_recv.at[r, c, y], *sems, at_y((y + k) % n_y))
        keep(pq_send.at[r, c], pq_recv.at[r, c, y], sems[1])

    def solve(r, c):
        wait_for(pq_recv.at[r, c], pq_recv_sem.at[r, c])
        low, high = jnp.zeros((8, 128), F32), jnp.zeros((8, 128), F32)
        for q in range(n_y):
            low = low + jnp.where(q < y, pq_recv[r, c, q, 0], 0.0)
            high = high + jnp.where(q > y, pq_recv[r, c, q, 1], 0.0)
        for j in range(line):
            low = low + cols[0, j : j + 1] * fin[r, c, j]
            xs[r, c, j] = cols[1, j : j + 1] * low
        for j in reversed(range(line)):
            xs[r, c, j] = xs[r, c, j] + cols[0, j : j + 1] * high
            high = high + cols[1, j : j + 1] * fin[r, c, j]
        spot_there = piece(ext.at[r, c], i, 8)
        sems = out_send_sem.at[r, c], out_recv_sem.at[r, c]
        each_on_line(lambda j: send(xs.at[r, c, j], spot_there, *sems, at_line(j)))
        keep(xs.at[r, c, i], spot_there, sems[1])

    def send_halo(r, c):
        wait_for(ext.at[r, c, pl.ds(8, rows)], out_recv_sem.at[r, c])
        which = ([2 + c, 0, 1] if c == 0 else [2 + c]) if r == 0 else []
        for side, other, near, edge in ((0, before, 8, 8), (1, after, last - 2, last - 1)):
            halo_send[r, c, side, 0:2, :] = ext[r, c, near : near + 2, :]
            for k, w in enumerate(which):
                halo_send[r, c, side, 2 + k : 3 + k, :] = coef[w, edge : edge + 1, :]
            send(
                halo_send.at[r, c, side], halo_recv.at[r, c, side],
                halo_send_sem.at[r, c], halo_recv_sem.at[r, c], at_tile(other),
            )

    def relax(r, c):
        wait_for(halo_recv.at[r, c], halo_recv_sem.at[r, c])
        above = jnp.where(t > 0, halo_recv[r, c, 1], 0.0)
        below = jnp.where(t < n_tile - 1, halo_recv[r, c, 0], 0.0)
        ext[r, c, 6:8, :] = above[0:2]
        ext[r, c, last : last + 2, :] = below[0:2]
        which = ([2 + c, 0, 1] if c == 0 else [2 + c]) if r == 0 else []
        for k, w in enumerate(which):
            coef[w, 7:8, :] = above[2 + k : 3 + k]
            coef[w, last : last + 1, :] = below[2 + k : 3 + k]
        height = rows + 16
        column = iota((height, width), 1)
        v = ext[r, c]
        for _ in range(2):
            left = jnp.where(column == 0, 0.0, pltpu.roll(v, 1, 1))
            right = jnp.where(column == width - 1, 0.0, pltpu.roll(v, width - 1, 1))
            around = (pltpu.roll(v, 1, 0) + pltpu.roll(v, height - 1, 0)) + (left + right)
            v = coef[1] * v + (coef[0] * around + coef[2 + c])
        fld[r, c] = v[8:last]

    forward_slots()
    forward_matches(0)
    totals(0, 0)
    totals(0, 1)
    solve(0, 0)
    forward_matches(1)
    solve(0, 1)
    chosen = choose()
    place_matches(0, chosen)
    send_halo(0, 0)
    relax(0, 0)
    send_in(fld.at[0, 0], 1, 0)
    place_matches(1, chosen)
    send_halo(0, 1)
    totals(1, 0)
    relax(0, 1)
    send_in(fld.at[0, 1], 1, 1)
    solve(1, 0)
    totals(1, 1)
    solve(1, 1)
    for c in range(2):
        send_halo(1, c)
        relax(1, c)
        keep(fld.at[1, c], out_ref.at[0, c], store_sem.at[c])

    for c in range(2):
        for r in range(2):
            wait_for(fin.at[r, c, pl.ds(0, line - 1)], fin_send_sem.at[r, c])
            wait_for(xs.at[r, c, pl.ds(0, line - 1)], out_send_sem.at[r, c])
            wait_for(pq_recv.at[r, c, pl.ds(0, n_y - 1)], pq_send_sem.at[r, c])
            wait_for(halo_send.at[r, c], halo_send_sem.at[r, c])
        wait_for(ma_send.at[c, pl.ds(0, n_y - 1)], ma_send_sem.at[c])
        wait_for(mb_recv.at[c, pl.ds(0, line - 1)], mb_send_sem.at[c])
    wait_for(sa_send.at[pl.ds(0, n_y - 1)], sa_send_sem)
    wait_for(sb_recv.at[pl.ds(0, line - 1)], sb_send_sem)
    for c in range(2):
        pltpu.make_async_copy(fld.at[1, c], out_ref.at[0, c], store_sem.at[c]).wait()


def local(n_sec, n_tile, node_flow, classes, table, z_couple, match_dest, match_slot, match_vectors):
    _, comps, rows, width = node_flow.shape
    line = rows * width // 1024
    n_y = n_sec // line
    matches = match_vectors.shape[0]
    vmem, dma = pltpu.VMEM, pltpu.SemaphoreType.DMA
    z = jnp.pad(z_couple, (0, 128 - n_sec), constant_values=26.0).reshape(1, 128)
    return pl.pallas_call(
        functools.partial(kernel, (n_y, line, n_tile, rows, width)),
        out_shape=jax.ShapeDtypeStruct(node_flow.shape, F32),
        in_specs=[pl.BlockSpec(memory_space=pl.ANY)] * 7,
        out_specs=pl.BlockSpec(memory_space=pl.ANY),
        scratch_shapes=[
            vmem((2, 2, line, 8, 128), F32),
            vmem((2, 2, line, 8, 128), F32),
            vmem((2, 2, rows + 16, width), F32),
            vmem((2, 2, rows, width), F32),
            vmem((2, 2, 2, 8, 128), F32),
            vmem((2, 2, n_y, 2, 8, 128), F32),
            vmem((2, line, 128), F32),
            vmem((2, n_y, line, CAP, 128), F32),
            vmem((2, n_y, line, CAP, 128), F32),
            vmem((2, line, n_y, CAP, 128), F32),
            vmem((n_y, line, 128), F32),
            vmem((n_y, line, 128), F32),
            vmem((line, 1, 128), F32),
            vmem((line, 1, 128), F32),
            vmem((2, 2, 2, 8, width), F32),
            vmem((2, 2, 2, 8, width), F32),
            vmem((4, rows + 16, width), F32),
            vmem((rows, width), jnp.int32),
            vmem((matches, 256), F32),
            vmem((1, 128), F32),
            vmem((1, matches), jnp.int32),
            vmem((1, matches), jnp.int32),
            pltpu.SMEM((table.shape[0],), F32),
            dma((6,)),
            *([dma((2, 2))] * 8),
            *([dma((2,))] * 4),
            *([dma(())] * 4),
            dma((2,)),
        ],
        compiler_params=pltpu.CompilerParams(
            collective_id=0, has_side_effects=True, vmem_limit_bytes=VMEM_LIMIT
        ),
        cost_estimate=pl.CostEstimate(flops=10**9, bytes_accessed=10**6, transcendentals=0),
        name="align",
    )(
        node_flow,
        classes,
        table,
        z,
        match_dest.reshape(1, matches),
        match_slot.reshape(1, matches),
        match_vectors,
    )


def solution(mesh):
    return jax.shard_map(
        functools.partial(local, mesh.shape["sec"], mesh.shape["tile"]),
        mesh=mesh,
        in_specs=(
            P("sec", None, "tile", None),
            P("sec", "tile", None),
            P(),
            P(),
            P(("sec", "tile"), None),
            P(("sec", "tile")),
            P(("sec", "tile"), None),
        ),
        out_specs=P("sec", None, "tile", None),
        check_vma=False,
    )
```

time: 118 us -> 101 us (0.86)
  Pallas kernels: 114 us -> 98.9 us
  local copies, waits for them, and re-layouts: 4.21 us -> 1.67 us
    pallas_call x1, Pallas kernels: 114 us -> 98.9 us  [local(): pl.pallas_call(functools.partial(kernel, (n_y, line, n_tile, rows, width)...]
    unnamed x15 -> x1, local copies, waits for them, and re-layouts: 4.21 us -> 1.67 us
where the time goes in v2:
time: 101 us
  Pallas kernels  98.9 us (98%)
  local copies, waits for them, and re-layouts  1.67 us (2%)
    pallas_call x1, Pallas kernels, local(): pl.pallas_call(functools.partial(kernel, (n_y, line, n_tile, rows, width)...  98.9 us

profile of v2, /device:TPU:1, one launch (start us, length us, event | category | flops | bytes accessed | tf_op | source)
XLA Modules:
  0.0 100.5 jit_solution(5689817455189565941)
XLA Ops:
  0.0 98.9 %align.1 = f32[1,2,64,512]{3,2,1,0:T(8,128)} custom-call(f32[1,2,64,512]{3,2,1,0:T(8,128)} %node_ref.1, s32[1,64,512]{2,1,0:T(8,128)} %classes_ref.1, f32[8]{0:T(128)} %table_ref.1, f32[1,128]{1,0:T(1,128)} %bitcast.5, s32[1,256]{1,0:T(1,128)} %bitcast.3, s32[1,256]{1,0:T(1,128)} %bitcast.4, f32[256,256]{1,0:T(8,128)} %vec_ref.1), custom_call_target="tpu_custom_call" | custom-call | flops 1000000000 | bytes 1000000 | tf_op jit(solution)/shard_map/align/pallas_call | solution.py:353
  98.9 1.7 %copy.9 = f32[1,2,64,512]{3,2,1,0:T(8,128)} copy(f32[1,2,64,512]{3,2,1,0:T(8,128)} %align.1) | data formatting | bytes 524288

commit v3 on v2

--- a/solution.py
+++ b/solution.py
@@ -60,15 +60,16 @@
     node_ref, classes_ref, table_ref, z_ref, dest_ref, slot_ref, vec_ref, out_ref,
     fin, xs, ext, fld, pq_send, pq_recv, cols,
     ma_send, ma_recv, mb_recv, sa_send, sa_recv, sb_send, sb_recv,
-    halo_send, halo_recv, coef, cls, vec, z_own, dest_own, slot_own, table,
+    edge_send, edge_recv, side_send, side_recv, coef, cls, vec, z_own, dest_own, slot_own, table,
     load_sem, fin_send_sem, fin_recv_sem, pq_send_sem, pq_recv_sem, out_send_sem, out_recv_sem,
-    halo_send_sem, halo_recv_sem, ma_send_sem, ma_recv_sem, mb_send_sem, mb_recv_sem,
+    edge_send_sem, edge_recv_sem, side_send_sem, side_recv_sem, ma_send_sem, ma_recv_sem, mb_send_sem, mb_recv_sem,
     sa_send_sem, sa_recv_sem, sb_send_sem, sb_recv_sem, store_sem,
 ):
     n_y, line, n_tile, rows, width = dims
     n_sec = n_y * line
     per_row = width // 128
     last = rows + 8
+    tops = rows // 8
     sec, t = lax.axis_index("sec"), lax.axis_index("tile")
     y, i = sec // line, sec % line
 
@@ -128,17 +129,23 @@
         greet(at_y((y + k) % n_y))
     for s in (before, after):
         greet(at_tile(s))
+    for k in range(per_row):
+        greet((y * line + k * tops, after))
+        greet((y * line + k * tops + 1 % tops, before))
 
     ext[:, :, 0:8, :] = jnp.zeros((2, 2, 8, width), F32)
     ext[:, :, last:, :] = jnp.zeros((2, 2, 8, width), F32)
     coef[:, 0:8, :] = jnp.zeros((4, 8, width), F32)
     coef[:, last:, :] = jnp.zeros((4, 8, width), F32)
 
-    pl.semaphore_wait(barrier, line - 1 + n_y - 1 + 2)
+    on_top = i % tops == 0
+    on_bottom = i % tops == 1 % tops
+    edges = on_top.astype(jnp.int32) + on_bottom.astype(jnp.int32)
+    pl.semaphore_wait(barrier, line - 1 + n_y - 1 + 2 + line * edges)
 
     def piece(field, j, base):
-        top = pl.multiple_of(base + (j // per_row) * 8, 8)
-        left = pl.multiple_of((j % per_row) * 128, 128)
+        top = pl.multiple_of(base + (tops - j % tops) % tops * 8, 8)
+        left = pl.multiple_of(j // tops * 128, 128)
         return field.at[pl.ds(top, 8), pl.ds(left, 128)]
 
     def send_in(field, r, c):
@@ -269,31 +276,61 @@
             high = high + cols[1, j : j + 1] * fin[r, c, j]
         spot_there = piece(ext.at[r, c], i, 8)
         sems = out_send_sem.at[r, c], out_recv_sem.at[r, c]
-        each_on_line(lambda j: send(xs.at[r, c, j], spot_there, *sems, at_line(j)))
+        for side, here in ((0, on_top), (1, on_bottom)):
+
+            @pl.when(here)
+            def _():
+                for j in range(line):
+                    edge_send[r, c, side, j] = xs[r, c, j, 6 * side : 6 * side + 2]
+
+        def over(j, side, beyond):
+            send(
+                edge_send.at[r, c, side, j], edge_recv.at[r, c, side, i // tops],
+                edge_send_sem.at[r, c, side], edge_recv_sem.at[r, c, side], (y * line + j, beyond),
+            )
+
+        def both(j):
+            for side, here, beyond in ((0, on_top, before), (1, on_bottom, after)):
+
+                @pl.when(here)
+                def _():
+                    over(j, side, beyond)
+
+            send(xs.at[r, c, j], spot_there, *sems, at_line(j))
+
+        each_on_line(both)
+        for side, here, beyond in ((0, on_top, before), (1, on_bottom, after)):
+
+            @pl.when(here)
+            def _():
+                over(i, side, beyond)
+
         keep(xs.at[r, c, i], spot_there, sems[1])
 
-    def send_halo(r, c):
+    def send_sides(c):
+        which = [2, 0, 1] if c == 0 else [3]
+        for side, other, edge in ((0, before, 8), (1, after, last - 1)):
+            for k, w in enumerate(which):
+                side_send[c, side, k : k + 1, :] = coef[w, edge : edge + 1, :]
+            send(
+                side_send.at[c, side], side_recv.at[c, side], side_send_sem.at[c], side_recv_sem.at[c], at_tile(other)
+            )
+
+    def relax(r, c):
+        if r == 0:
+            wait_for(side_recv.at[c], side_recv_sem.at[c])
+            above = jnp.where(t > 0, side_recv[c, 1], 0.0)
+            below = jnp.where(t < n_tile - 1, side_recv[c, 0], 0.0)
+            for k, w in enumerate([2, 0, 1] if c == 0 else [3]):
+                coef[w, 7:8, :] = above[k : k + 1]
+                coef[w, last : last + 1, :] = below[k : k + 1]
+        for side in range(2):
+            wait_for(edge_recv.at[r, c, side], edge_recv_sem.at[r, c, side])
+        for b in range(per_row):
+            lanes = slice(b * 128, (b + 1) * 128)
+            ext[r, c, 6:8, lanes] = jnp.where(t > 0, edge_recv[r, c, 1, b], 0.0)
+            ext[r, c, last : last + 2, lanes] = jnp.where(t < n_tile - 1, edge_recv[r, c, 0, b], 0.0)
         wait_for(ext.at[r, c, pl.ds(8, rows)], out_recv_sem.at[r, c])
-        which = ([2 + c, 0, 1] if c == 0 else [2 + c]) if r == 0 else []
-        for side, other, near, edge in ((0, before, 8, 8), (1, after, last - 2, last - 1)):
-            halo_send[r, c, side, 0:2, :] = ext[r, c, near : near + 2, :]
-            for k, w in enumerate(which):
-                halo_send[r, c, side, 2 + k : 3 + k, :] = coef[w, edge : edge + 1, :]
-            send(
-                halo_send.at[r, c, side], halo_recv.at[r, c, side],
-                halo_send_sem.at[r, c], halo_recv_sem.at[r, c], at_tile(other),
-            )
-
-    def relax(r, c):
-        wait_for(halo_recv.at[r, c], halo_recv_sem.at[r, c])
-        above = jnp.where(t > 0, halo_recv[r, c, 1], 0.0)
-        below = jnp.where(t < n_tile - 1, halo_recv[r, c, 0], 0.0)
-        ext[r, c, 6:8, :] = above[0:2]
-        ext[r, c, last : last + 2, :] = below[0:2]
-        which = ([2 + c, 0, 1] if c == 0 else [2 + c]) if r == 0 else []
-        for k, w in enumerate(which):
-            coef[w, 7:8, :] = above[2 + k : 3 + k]
-            coef[w, last : last + 1, :] = below[2 + k : 3 + k]
         height = rows + 16
         column = iota((height, width), 1)
         v = ext[r, c]
@@ -304,8 +341,8 @@
             v = coef[1] * v + (coef[0] * around + coef[2 + c])
         fld[r, c] = v[8:last]
 
+    forward_matches(0)
     forward_slots()
-    forward_matches(0)
     totals(0, 0)
     totals(0, 1)
     solve(0, 0)
@@ -313,19 +350,18 @@
     solve(0, 1)
     chosen = choose()
     place_matches(0, chosen)
-    send_halo(0, 0)
+    send_sides(0)
     relax(0, 0)
     send_in(fld.at[0, 0], 1, 0)
     place_matches(1, chosen)
-    send_halo(0, 1)
-    totals(1, 0)
+    send_sides(1)
     relax(0, 1)
     send_in(fld.at[0, 1], 1, 1)
+    totals(1, 0)
     solve(1, 0)
     totals(1, 1)
     solve(1, 1)
     for c in range(2):
-        send_halo(1, c)
         relax(1, c)
         keep(fld.at[1, c], out_ref.at[0, c], store_sem.at[c])
 
@@ -334,9 +370,15 @@
             wait_for(fin.at[r, c, pl.ds(0, line - 1)], fin_send_sem.at[r, c])
             wait_for(xs.at[r, c, pl.ds(0, line - 1)], out_send_sem.at[r, c])
             wait_for(pq_recv.at[r, c, pl.ds(0, n_y - 1)], pq_send_sem.at[r, c])
-            wait_for(halo_send.at[r, c], halo_send_sem.at[r, c])
+            for side, here in ((0, on_top), (1, on_bottom)):
+
+                @pl.when(here)
+                def _():
+                    wait_for(edge_send.at[r, c, side], edge_send_sem.at[r, c, side])
+
         wait_for(ma_send.at[c, pl.ds(0, n_y - 1)], ma_send_sem.at[c])
         wait_for(mb_recv.at[c, pl.ds(0, line - 1)], mb_send_sem.at[c])
+        wait_for(side_send.at[c], side_send_sem.at[c])
     wait_for(sa_send.at[pl.ds(0, n_y - 1)], sa_send_sem)
     wait_for(sb_recv.at[pl.ds(0, line - 1)], sb_send_sem)
     for c in range(2):
@@ -370,8 +412,10 @@
             vmem((n_y, line, 128), F32),
             vmem((line, 1, 128), F32),
             vmem((line, 1, 128), F32),
-            vmem((2, 2, 2, 8, width), F32),
-            vmem((2, 2, 2, 8, width), F32),
+            vmem((2, 2, 2, line, 2, 128), F32),
+            vmem((2, 2, 2, width // 128, 2, 128), F32),
+            vmem((2, 2, 8, width), F32),
+            vmem((2, 2, 8, width), F32),
             vmem((4, rows + 16, width), F32),
             vmem((rows, width), jnp.int32),
             vmem((matches, 256), F32),
@@ -380,8 +424,9 @@
             vmem((1, matches), jnp.int32),
             pltpu.SMEM((table.shape[0],), F32),
             dma((6,)),
-            *([dma((2, 2))] * 8),
-            *([dma((2,))] * 4),
+            *([dma((2, 2))] * 6),
+            *([dma((2, 2, 2))] * 2),
+            *([dma((2,))] * 6),
             *([dma(())] * 4),
             dma((2,)),
         ],

time: 101 us -> 96.3 us (0.953)
  Pallas kernels: 98.9 us -> 94.5 us
    pallas_call x1, Pallas kernels: 98.9 us -> 94.5 us  [local(): pl.pallas_call(functools.partial(kernel, (n_y, line, n_tile, rows, width)...]
where the time goes in v3:
time: 96.3 us; the launch traced here: 96.1 us
  Pallas kernels  94.5 us (98%)
  local copies, waits for them, and re-layouts  1.67 us (2%)
    pallas_call x1, Pallas kernels, local(): pl.pallas_call(functools.partial(kernel, (n_y, line, n_tile, rows, width)...  94.5 us

profile of v3, /device:TPU:1, one launch (start us, length us, event | category | flops | bytes accessed | tf_op | source)
XLA Modules:
  0.0 96.1 jit_solution(17143496264620218771)
XLA Ops:
  0.0 94.5 %align.1 = f32[1,2,64,512]{3,2,1,0:T(8,128)} custom-call(f32[1,2,64,512]{3,2,1,0:T(8,128)} %node_ref.1, s32[1,64,512]{2,1,0:T(8,128)} %classes_ref.1, f32[8]{0:T(128)} %table_ref.1, f32[1,128]{1,0:T(1,128)} %bitcast.5, s32[1,256]{1,0:T(1,128)} %bitcast.3, s32[1,256]{1,0:T(1,128)} %bitcast.4, f32[256,256]{1,0:T(8,128)} %vec_ref.1), custom_call_target="tpu_custom_call" | custom-call | flops 1000000000 | bytes 1000000 | tf_op jit(solution)/shard_map/align/pallas_call | solution.py:395
  94.5 1.7 %copy.9 = f32[1,2,64,512]{3,2,1,0:T(8,128)} copy(f32[1,2,64,512]{3,2,1,0:T(8,128)} %align.1) | data formatting | bytes 524288

commit v4 on v3

--- a/solution.py
+++ b/solution.py
@@ -90,6 +90,13 @@
         def _(k):
             act((i + half + k) % line)
             act((i + half - k) % line)
+
+    def each_from_first(act):
+        @pl.loop(0, line)
+        def _(j):
+            @pl.when(j != i)
+            def _():
+                act(j)
 
     def send(src, dst, send_sem, recv_sem, device):
         pltpu.make_async_remote_copy(
@@ -298,7 +305,8 @@
 
             send(xs.at[r, c, j], spot_there, *sems, at_line(j))
 
-        each_on_line(both)
+        order = each_from_first if (r, c) in ((1, 1),) else each_on_line
+        order(both)
         for side, here, beyond in ((0, on_top, before), (1, on_bottom, after)):
 
             @pl.when(here)

time: 96.3 us -> 95.4 us (level)
  no operation moved by 1% of the time
where the time goes in v4:
time: 95.4 us; the launch traced here: 95.2 us
  Pallas kernels  93.6 us (98%)
  local copies, waits for them, and re-layouts  1.67 us (2%)
    pallas_call x1, Pallas kernels, local(): pl.pallas_call(functools.partial(kernel, (n_y, line, n_tile, rows, width)...  93.6 us

profile of v4, /device:TPU:1, one launch (start us, length us, event | category | flops | bytes accessed | tf_op | source)
XLA Modules:
  0.0 95.2 jit_solution(17297053014312178505)
XLA Ops:
  0.0 93.6 %align.1 = f32[1,2,64,512]{3,2,1,0:T(8,128)} custom-call(f32[1,2,64,512]{3,2,1,0:T(8,128)} %node_ref.1, s32[1,64,512]{2,1,0:T(8,128)} %classes_ref.1, f32[8]{0:T(128)} %table_ref.1, f32[1,128]{1,0:T(1,128)} %bitcast.5, s32[1,256]{1,0:T(1,128)} %bitcast.3, s32[1,256]{1,0:T(1,128)} %bitcast.4, f32[256,256]{1,0:T(8,128)} %vec_ref.1), custom_call_target="tpu_custom_call" | custom-call | flops 1000000000 | bytes 1000000 | tf_op jit(solution)/shard_map/align/pallas_call | solution.py:403
  93.6 1.7 %copy.9 = f32[1,2,64,512]{3,2,1,0:T(8,128)} copy(f32[1,2,64,512]{3,2,1,0:T(8,128)} %align.1) | data formatting | bytes 524288

commit v5 on v4

--- a/solution.py
+++ b/solution.py
@@ -351,10 +351,10 @@
 
     forward_matches(0)
     forward_slots()
+    forward_matches(1)
     totals(0, 0)
     totals(0, 1)
     solve(0, 0)
-    forward_matches(1)
     solve(0, 1)
     chosen = choose()
     place_matches(0, chosen)

time: 95.4 us -> 94.3 us (0.988)
  Pallas kernels: 93.6 us -> 92.5 us
    pallas_call x1, Pallas kernels: 93.6 us -> 92.5 us  [local(): pl.pallas_call(functools.partial(kernel, (n_y, line, n_tile, rows, width)...]
where the time goes in v5:
time: 94.3 us; the launch traced here: 94.2 us
  Pallas kernels  92.5 us (98%)
  local copies, waits for them, and re-layouts  1.67 us (2%)
    pallas_call x1, Pallas kernels, local(): pl.pallas_call(functools.partial(kernel, (n_y, line, n_tile, rows, width)...  92.5 us

profile of v5, /device:TPU:1, one launch (start us, length us, event | category | flops | bytes accessed | tf_op | source)
XLA Modules:
  0.0 94.2 jit_solution(4578544791921410359)
XLA Ops:
  0.0 92.5 %align.1 = f32[1,2,64,512]{3,2,1,0:T(8,128)} custom-call(f32[1,2,64,512]{3,2,1,0:T(8,128)} %node_ref.1, s32[1,64,512]{2,1,0:T(8,128)} %classes_ref.1, f32[8]{0:T(128)} %table_ref.1, f32[1,128]{1,0:T(1,128)} %bitcast.5, s32[1,256]{1,0:T(1,128)} %bitcast.3, s32[1,256]{1,0:T(1,128)} %bitcast.4, f32[256,256]{1,0:T(8,128)} %vec_ref.1), custom_call_target="tpu_custom_call" | custom-call | flops 1000000000 | bytes 1000000 | tf_op jit(solution)/shard_map/align/pallas_call | solution.py:403
  92.5 1.7 %copy.9 = f32[1,2,64,512]{3,2,1,0:T(8,128)} copy(f32[1,2,64,512]{3,2,1,0:T(8,128)} %align.1) | data formatting | bytes 524288

commit v6 on v5

--- a/solution.py
+++ b/solution.py
@@ -265,7 +265,7 @@
             low, high = low + cols[0, j : j + 1] * f, high + cols[1, j : j + 1] * f
         pq_send[r, c, 0], pq_send[r, c, 1] = low, high
         sems = pq_send_sem.at[r, c], pq_recv_sem.at[r, c]
-        for k in range(1, n_y):
+        for k in sorted(range(1, n_y), key=lambda k: -min(k, n_y - k)):
             send(pq_send.at[r, c], pq_recv.at[r, c, y], *sems, at_y((y + k) % n_y))
         keep(pq_send.at[r, c], pq_recv.at[r, c, y], sems[1])
 
@@ -353,16 +353,16 @@
     forward_slots()
     forward_matches(1)
     totals(0, 0)
+    solve(0, 0)
     totals(0, 1)
-    solve(0, 0)
     solve(0, 1)
     chosen = choose()
     place_matches(0, chosen)
     send_sides(0)
+    place_matches(1, chosen)
+    send_sides(1)
     relax(0, 0)
     send_in(fld.at[0, 0], 1, 0)
-    place_matches(1, chosen)
-    send_sides(1)
     relax(0, 1)
     send_in(fld.at[0, 1], 1, 1)
     totals(1, 0)

time: 94.3 us -> 94.9 us (level)
  no operation moved by 1% of the time
where the time goes in v6:
time: 94.9 us; the launch traced here: 94.8 us
  Pallas kernels  93.1 us (98%)
  local copies, waits for them, and re-layouts  1.67 us (2%)
    pallas_call x1, Pallas kernels, local(): pl.pallas_call(functools.partial(kernel, (n_y, line, n_tile, rows, width)...  93.1 us

profile of v6, /device:TPU:1, one launch (start us, length us, event | category | flops | bytes accessed | tf_op | source)
XLA Modules:
  0.0 94.8 jit_solution(14005071810644376582)
XLA Ops:
  0.0 93.1 %align.1 = f32[1,2,64,512]{3,2,1,0:T(8,128)} custom-call(f32[1,2,64,512]{3,2,1,0:T(8,128)} %node_ref.1, s32[1,64,512]{2,1,0:T(8,128)} %classes_ref.1, f32[8]{0:T(128)} %table_ref.1, f32[1,128]{1,0:T(1,128)} %bitcast.5, s32[1,256]{1,0:T(1,128)} %bitcast.3, s32[1,256]{1,0:T(1,128)} %bitcast.4, f32[256,256]{1,0:T(8,128)} %vec_ref.1), custom_call_target="tpu_custom_call" | custom-call | flops 1000000000 | bytes 1000000 | tf_op jit(solution)/shard_map/align/pallas_call | solution.py:403
  93.1 1.7 %copy.9 = f32[1,2,64,512]{3,2,1,0:T(8,128)} copy(f32[1,2,64,512]{3,2,1,0:T(8,128)} %align.1) | data formatting | bytes 524288
